TPU v7x, 128 devices: a whole 4x4x4 slice. The times are simulated.
128 devices in a mesh: wide: 32 (over y, x, z_hi), blk: 4 (over z_lo, core).
Axes of the slice: x: 4, y: 4, z: 4 (z_hi: 2, z_lo: 2; z = z_hi * 2 + z_lo), core: 2. Of those that a mesh axis runs over, the one named last changes fastest.
Arguments:
- visual_features: bfloat16 [131072, 1152], P(('wide', 'blk')), may hold values from -0.1875 to 0.1875
- sentence_features: bfloat16 [4096, 1152], P(('wide', 'blk')), may hold values from -0.1875 to 0.1875
- true_partner_ids: int32 [131072], P(('wide', 'blk')), may hold values from 0 to 4095
- inverse_warmth: float32 [], replicated, may hold values from 90 to 110
- additive_adjust: float32 [], replicated, may hold values from -12 to -9
Outputs:
- grad_images: float32 [131072, 1152], P(('wide', 'blk'))
- grad_texts: float32 [4096, 1152], P(('wide', 'blk'))
Inputs may be any that keep to these rules, and one draw needn't show every extreme that they name: Image i is paired with text true_partner_ids[i]; a text may be paired with several images or none.
All inputs are finite; a program needn't handle non-finite values.
Results may differ from a plain program's by a relative error of at most 0.007.
Values may be sent and summed in bfloat16 or wider, within the bound.
A program may use at most 64 MiB of HBM per device.

v0:
```python
import jax
import jax.numpy as jnp
from jax import lax
from jax.sharding import PartitionSpec as P


def passed_along(array, axis, by):
    peers = lax.axis_size(axis)
    return lax.ppermute(array, axis, [(i, (i + by) % peers) for i in range(peers)])


def remaining_factors(
    visual_features, tile_length, true_partner_ids, leading_offset, inverse_warmth, additive_adjust
):
    cosine_grid = lax.dot_general(
        visual_features, tile_length, (((1,), (1,)), ((), ())), preferred_element_type=jnp.float32
    )
    sigmoid_levels = inverse_warmth * cosine_grid + additive_adjust
    columns = leading_offset + lax.iota(jnp.int32, tile_length.shape[0])
    plus_minus_ones = jnp.where(true_partner_ids[:, None] == columns[None, :], 1.0, -1.0).astype(
        jnp.float32
    )
    return (
        -inverse_warmth * plus_minus_ones * jax.nn.sigmoid(-plus_minus_ones * sigmoid_levels)
    ).astype(jnp.bfloat16)


def both_grads(visual_features, tile_length, loss_grid_scaled):
    incoming_grad_part = jnp.dot(loss_grid_scaled, tile_length, preferred_element_type=jnp.float32)
    returned_grad_part = lax.dot_general(
        loss_grid_scaled,
        visual_features,
        (((0,), (0,)), ((), ())),
        preferred_element_type=jnp.float32,
    )
    return (incoming_grad_part, returned_grad_part)


def shards(visual_features, sentence_features, true_partner_ids, inverse_warmth, additive_adjust):
    width = visual_features.shape[1]
    tdev = sentence_features.shape[0]
    n_wide = lax.axis_size("wide")
    n_blk = lax.axis_size("blk")
    wpos = lax.axis_index("wide")
    caption_group = tdev * n_blk
    held_start = jnp.zeros((tdev, width), jnp.float32)

    def step(turn, carry):
        grad_img, tile_length, held = carry
        reference_offset = (wpos - turn) % n_wide
        joined_tiles = lax.all_gather(tile_length, "blk", axis=0, tiled=True)
        loss_grid_scaled = remaining_factors(
            visual_features,
            joined_tiles,
            true_partner_ids,
            reference_offset * caption_group,
            inverse_warmth,
            additive_adjust,
        )
        incoming_grad_part, returned_grad_part = both_grads(
            visual_features, joined_tiles, loss_grid_scaled
        )
        grad_img = grad_img + incoming_grad_part
        held = held + lax.psum_scatter(
            returned_grad_part.astype(jnp.bfloat16), "blk", scatter_dimension=0, tiled=True
        ).astype(jnp.float32)
        held = passed_along(held, "wide", 1)
        tile_length = passed_along(tile_length, "wide", 1)
        return (grad_img, tile_length, held)

    start = (jnp.zeros(visual_features.shape, jnp.float32), sentence_features, held_start)
    grad_images, span_home, held = lax.fori_loop(0, n_wide, step, start)
    return (grad_images, held)


def solution(mesh):
    return jax.shard_map(
        shards,
        mesh=mesh,
        in_specs=(P(("wide", "blk"), None), P(("wide", "blk"), None), P(("wide", "blk")), P(), P()),
        out_specs=(P(("wide", "blk"), None), P(("wide", "blk"), None)),
        check_vma=False,
    )
```

profile of v0, /device:TPU:1, one launch (start us, length us, event | category | flops | bytes accessed | tf_op | source)
XLA Modules:
  0.0 1250.5 jit_solution(10544662852976132055)
XLA Ops:
  8.7 1234.5 %while.20 = (s32[]{:T(128)}, f32[1024,1152]{1,0:T(8,128)}, bf16[32,1152]{1,0:T(8,128)(2,1)S(1)}, f32[32,1152]{1,0:T(8,128)S(1)}, f32[]{:T(128)}, /*index=5*/s32[...) while((s32[]{:T(128)}, f32[1024,1152]{1,0:T(8,128)}, ...), condition=%wide.region_2.3_spmd.clone, body=%wide.region_0.2_spmd.clone.sunk | while | flops 910123136 | bytes 28145088 | solution.py:72
  25.2 16.2 %reduce-scatter.2.cloned.1.call-done = bf16[32,1152]{1,0:T(8,128)(2,1)} async-done(((bf16[128,1152]{1,0:T(8,128)(2,1)}), bf16[32,1152]{1,0:T(8,128)(2,1)}) %reduce-scatter.2.cloned.1.call-update) | async-done | bytes 73744 | tf_op jit(solution)/shard_map/while/body/eval_jaxpr/reduce_scatter | solution.py:64
  65.5 14.4 %reduce-scatter.2.cloned.1.call-done = bf16[32,1152]{1,0:T(8,128)(2,1)} async-done(((bf16[128,1152]{1,0:T(8,128)(2,1)}), bf16[32,1152]{1,0:T(8,128)(2,1)}) %reduce-scatter.2.cloned.1.call-update) | async-done | bytes 73744 | tf_op jit(solution)/shard_map/while/body/eval_jaxpr/reduce_scatter | solution.py:64
  142.2 14.3 %reduce-scatter.2.cloned.1.call-done = bf16[32,1152]{1,0:T(8,128)(2,1)} async-done(((bf16[128,1152]{1,0:T(8,128)(2,1)}), bf16[32,1152]{1,0:T(8,128)(2,1)}) %reduce-scatter.2.cloned.1.call-update) | async-done | bytes 73744 | tf_op jit(solution)/shard_map/while/body/eval_jaxpr/reduce_scatter | solution.py:64
  180.6 14.3 %reduce-scatter.2.cloned.1.call-done = bf16[32,1152]{1,0:T(8,128)(2,1)} async-done(((bf16[128,1152]{1,0:T(8,128)(2,1)}), bf16[32,1152]{1,0:T(8,128)(2,1)}) %reduce-scatter.2.cloned.1.call-update) | async-done | bytes 73744 | tf_op jit(solution)/shard_map/while/body/eval_jaxpr/reduce_scatter | solution.py:64
  219.0 14.3 %reduce-scatter.2.cloned.1.call-done = bf16[32,1152]{1,0:T(8,128)(2,1)} async-done(((bf16[128,1152]{1,0:T(8,128)(2,1)}), bf16[32,1152]{1,0:T(8,128)(2,1)}) %reduce-scatter.2.cloned.1.call-update) | async-done | bytes 73744 | tf_op jit(solution)/shard_map/while/body/eval_jaxpr/reduce_scatter | solution.py:64
  257.4 14.3 %reduce-scatter.2.cloned.1.call-done = bf16[32,1152]{1,0:T(8,128)(2,1)} async-done(((bf16[128,1152]{1,0:T(8,128)(2,1)}), bf16[32,1152]{1,0:T(8,128)(2,1)}) %reduce-scatter.2.cloned.1.call-update) | async-done | bytes 73744 | tf_op jit(solution)/shard_map/while/body/eval_jaxpr/reduce_scatter | solution.py:64
  295.7 14.3 %reduce-scatter.2.cloned.1.call-done = bf16[32,1152]{1,0:T(8,128)(2,1)} async-done(((bf16[128,1152]{1,0:T(8,128)(2,1)}), bf16[32,1152]{1,0:T(8,128)(2,1)}) %reduce-scatter.2.cloned.1.call-update) | async-done | bytes 73744 | tf_op jit(solution)/shard_map/while/body/eval_jaxpr/reduce_scatter | solution.py:64
  334.1 14.3 %reduce-scatter.2.cloned.1.call-done = bf16[32,1152]{1,0:T(8,128)(2,1)} async-done(((bf16[128,1152]{1,0:T(8,128)(2,1)}), bf16[32,1152]{1,0:T(8,128)(2,1)}) %reduce-scatter.2.cloned.1.call-update) | async-done | bytes 73744 | tf_op jit(solution)/shard_map/while/body/eval_jaxpr/reduce_scatter | solution.py:64
  372.5 14.3 %reduce-scatter.2.cloned.1.call-done = bf16[32,1152]{1,0:T(8,128)(2,1)} async-done(((bf16[128,1152]{1,0:T(8,128)(2,1)}), bf16[32,1152]{1,0:T(8,128)(2,1)}) %reduce-scatter.2.cloned.1.call-update) | async-done | bytes 73744 | tf_op jit(solution)/shard_map/while/body/eval_jaxpr/reduce_scatter | solution.py:64
  410.9 14.3 %reduce-scatter.2.cloned.1.call-done = bf16[32,1152]{1,0:T(8,128)(2,1)} async-done(((bf16[128,1152]{1,0:T(8,128)(2,1)}), bf16[32,1152]{1,0:T(8,128)(2,1)}) %reduce-scatter.2.cloned.1.call-update) | async-done | bytes 73744 | tf_op jit(solution)/shard_map/while/body/eval_jaxpr/reduce_scatter | solution.py:64
  449.3 14.3 %reduce-scatter.2.cloned.1.call-done = bf16[32,1152]{1,0:T(8,128)(2,1)} async-done(((bf16[128,1152]{1,0:T(8,128)(2,1)}), bf16[32,1152]{1,0:T(8,128)(2,1)}) %reduce-scatter.2.cloned.1.call-update) | async-done | bytes 73744 | tf_op jit(solution)/shard_map/while/body/eval_jaxpr/reduce_scatter | solution.py:64
  487.7 14.3 %reduce-scatter.2.cloned.1.call-done = bf16[32,1152]{1,0:T(8,128)(2,1)} async-done(((bf16[128,1152]{1,0:T(8,128)(2,1)}), bf16[32,1152]{1,0:T(8,128)(2,1)}) %reduce-scatter.2.cloned.1.call-update) | async-done | bytes 73744 | tf_op jit(solution)/shard_map/while/body/eval_jaxpr/reduce_scatter | solution.py:64
  526.0 14.3 %reduce-scatter.2.cloned.1.call-done = bf16[32,1152]{1,0:T(8,128)(2,1)} async-done(((bf16[128,1152]{1,0:T(8,128)(2,1)}), bf16[32,1152]{1,0:T(8,128)(2,1)}) %reduce-scatter.2.cloned.1.call-update) | async-done | bytes 73744 | tf_op jit(solution)/shard_map/while/body/eval_jaxpr/reduce_scatter | solution.py:64
  564.4 14.3 %reduce-scatter.2.cloned.1.call-done = bf16[32,1152]{1,0:T(8,128)(2,1)} async-done(((bf16[128,1152]{1,0:T(8,128)(2,1)}), bf16[32,1152]{1,0:T(8,128)(2,1)}) %reduce-scatter.2.cloned.1.call-update) | async-done | bytes 73744 | tf_op jit(solution)/shard_map/while/body/eval_jaxpr/reduce_scatter | solution.py:64
  602.8 14.3 %reduce-scatter.2.cloned.1.call-done = bf16[32,1152]{1,0:T(8,128)(2,1)} async-done(((bf16[128,1152]{1,0:T(8,128)(2,1)}), bf16[32,1152]{1,0:T(8,128)(2,1)}) %reduce-scatter.2.cloned.1.call-update) | async-done | bytes 73744 | tf_op jit(solution)/shard_map/while/body/eval_jaxpr/reduce_scatter | solution.py:64
  641.2 14.3 %reduce-scatter.2.cloned.1.call-done = bf16[32,1152]{1,0:T(8,128)(2,1)} async-done(((bf16[128,1152]{1,0:T(8,128)(2,1)}), bf16[32,1152]{1,0:T(8,128)(2,1)}) %reduce-scatter.2.cloned.1.call-update) | async-done | bytes 73744 | tf_op jit(solution)/shard_map/while/body/eval_jaxpr/reduce_scatter | solution.py:64
  679.6 14.3 %reduce-scatter.2.cloned.1.call-done = bf16[32,1152]{1,0:T(8,128)(2,1)} async-done(((bf16[128,1152]{1,0:T(8,128)(2,1)}), bf16[32,1152]{1,0:T(8,128)(2,1)}) %reduce-scatter.2.cloned.1.call-update) | async-done | bytes 73744 | tf_op jit(solution)/shard_map/while/body/eval_jaxpr/reduce_scatter | solution.py:64
  718.0 14.3 %reduce-scatter.2.cloned.1.call-done = bf16[32,1152]{1,0:T(8,128)(2,1)} async-done(((bf16[128,1152]{1,0:T(8,128)(2,1)}), bf16[32,1152]{1,0:T(8,128)(2,1)}) %reduce-scatter.2.cloned.1.call-update) | async-done | bytes 73744 | tf_op jit(solution)/shard_map/while/body/eval_jaxpr/reduce_scatter | solution.py:64
  756.3 14.3 %reduce-scatter.2.cloned.1.call-done = bf16[32,1152]{1,0:T(8,128)(2,1)} async-done(((bf16[128,1152]{1,0:T(8,128)(2,1)}), bf16[32,1152]{1,0:T(8,128)(2,1)}) %reduce-scatter.2.cloned.1.call-update) | async-done | bytes 73744 | tf_op jit(solution)/shard_map/while/body/eval_jaxpr/reduce_scatter | solution.py:64
  794.7 14.3 %reduce-scatter.2.cloned.1.call-done = bf16[32,1152]{1,0:T(8,128)(2,1)} async-done(((bf16[128,1152]{1,0:T(8,128)(2,1)}), bf16[32,1152]{1,0:T(8,128)(2,1)}) %reduce-scatter.2.cloned.1.call-update) | async-done | bytes 73744 | tf_op jit(solution)/shard_map/while/body/eval_jaxpr/reduce_scatter | solution.py:64
  833.1 14.3 %reduce-scatter.2.cloned.1.call-done = bf16[32,1152]{1,0:T(8,128)(2,1)} async-done(((bf16[128,1152]{1,0:T(8,128)(2,1)}), bf16[32,1152]{1,0:T(8,128)(2,1)}) %reduce-scatter.2.cloned.1.call-update) | async-done | bytes 73744 | tf_op jit(solution)/shard_map/while/body/eval_jaxpr/reduce_scatter | solution.py:64
  871.5 14.3 %reduce-scatter.2.cloned.1.call-done = bf16[32,1152]{1,0:T(8,128)(2,1)} async-done(((bf16[128,1152]{1,0:T(8,128)(2,1)}), bf16[32,1152]{1,0:T(8,128)(2,1)}) %reduce-scatter.2.cloned.1.call-update) | async-done | bytes 73744 | tf_op jit(solution)/shard_map/while/body/eval_jaxpr/reduce_scatter | solution.py:64
  909.9 14.3 %reduce-scatter.2.cloned.1.call-done = bf16[32,1152]{1,0:T(8,128)(2,1)} async-done(((bf16[128,1152]{1,0:T(8,128)(2,1)}), bf16[32,1152]{1,0:T(8,128)(2,1)}) %reduce-scatter.2.cloned.1.call-update) | async-done | bytes 73744 | tf_op jit(solution)/shard_map/while/body/eval_jaxpr/reduce_scatter | solution.py:64
  948.3 14.3 %reduce-scatter.2.cloned.1.call-done = bf16[32,1152]{1,0:T(8,128)(2,1)} async-done(((bf16[128,1152]{1,0:T(8,128)(2,1)}), bf16[32,1152]{1,0:T(8,128)(2,1)}) %reduce-scatter.2.cloned.1.call-update) | async-done | bytes 73744 | tf_op jit(solution)/shard_map/while/body/eval_jaxpr/reduce_scatter | solution.py:64
  986.6 14.3 %reduce-scatter.2.cloned.1.call-done = bf16[32,1152]{1,0:T(8,128)(2,1)} async-done(((bf16[128,1152]{1,0:T(8,128)(2,1)}), bf16[32,1152]{1,0:T(8,128)(2,1)}) %reduce-scatter.2.cloned.1.call-update) | async-done | bytes 73744 | tf_op jit(solution)/shard_map/while/body/eval_jaxpr/reduce_scatter | solution.py:64
  1025.0 14.3 %reduce-scatter.2.cloned.1.call-done = bf16[32,1152]{1,0:T(8,128)(2,1)} async-done(((bf16[128,1152]{1,0:T(8,128)(2,1)}), bf16[32,1152]{1,0:T(8,128)(2,1)}) %reduce-scatter.2.cloned.1.call-update) | async-done | bytes 73744 | tf_op jit(solution)/shard_map/while/body/eval_jaxpr/reduce_scatter | solution.py:64
  1063.4 14.3 %reduce-scatter.2.cloned.1.call-done = bf16[32,1152]{1,0:T(8,128)(2,1)} async-done(((bf16[128,1152]{1,0:T(8,128)(2,1)}), bf16[32,1152]{1,0:T(8,128)(2,1)}) %reduce-scatter.2.cloned.1.call-update) | async-done | bytes 73744 | tf_op jit(solution)/shard_map/while/body/eval_jaxpr/reduce_scatter | solution.py:64
  1101.8 14.3 %reduce-scatter.2.cloned.1.call-done = bf16[32,1152]{1,0:T(8,128)(2,1)} async-done(((bf16[128,1152]{1,0:T(8,128)(2,1)}), bf16[32,1152]{1,0:T(8,128)(2,1)}) %reduce-scatter.2.cloned.1.call-update) | async-done | bytes 73744 | tf_op jit(solution)/shard_map/while/body/eval_jaxpr/reduce_scatter | solution.py:64
  1140.2 14.3 %reduce-scatter.2.cloned.1.call-done = bf16[32,1152]{1,0:T(8,128)(2,1)} async-done(((bf16[128,1152]{1,0:T(8,128)(2,1)}), bf16[32,1152]{1,0:T(8,128)(2,1)}) %reduce-scatter.2.cloned.1.call-update) | async-done | bytes 73744 | tf_op jit(solution)/shard_map/while/body/eval_jaxpr/reduce_scatter | solution.py:64
  1178.6 14.3 %reduce-scatter.2.cloned.1.call-done = bf16[32,1152]{1,0:T(8,128)(2,1)} async-done(((bf16[128,1152]{1,0:T(8,128)(2,1)}), bf16[32,1152]{1,0:T(8,128)(2,1)}) %reduce-scatter.2.cloned.1.call-update) | async-done | bytes 73744 | tf_op jit(solution)/shard_map/while/body/eval_jaxpr/reduce_scatter | solution.py:64
  1216.9 14.3 %reduce-scatter.2.cloned.1.call-done = bf16[32,1152]{1,0:T(8,128)(2,1)} async-done(((bf16[128,1152]{1,0:T(8,128)(2,1)}), bf16[32,1152]{1,0:T(8,128)(2,1)}) %reduce-scatter.2.cloned.1.call-update) | async-done | bytes 73744 | tf_op jit(solution)/shard_map/while/body/eval_jaxpr/reduce_scatter | solution.py:64
  (485 shorter events, 788.2 us)
Async XLA Ops:
  8.8 32.6 %reduce-scatter.2.cloned.1.call-start = ((), (), s32[]{:S(2)}) async-start(), calls=%async_computation.1 | async-start | bytes 368640 | tf_op jit(solution)/shard_map/while/body/eval_jaxpr/reduce_scatter | solution.py:64
  53.5 26.3 %reduce-scatter.2.cloned.1.call-start = ((), (), s32[]{:S(2)}) async-start(), calls=%async_computation.1 | async-start | bytes 368640 | tf_op jit(solution)/shard_map/while/body/eval_jaxpr/reduce_scatter | solution.py:64
  91.8 26.3 %reduce-scatter.2.cloned.1.call-start = ((), (), s32[]{:S(2)}) async-start(), calls=%async_computation.1 | async-start | bytes 368640 | tf_op jit(solution)/shard_map/while/body/eval_jaxpr/reduce_scatter | solution.py:64
  130.2 26.4 %reduce-scatter.2.cloned.1.call-start = ((), (), s32[]{:S(2)}) async-start(), calls=%async_computation.1 | async-start | bytes 368640 | tf_op jit(solution)/shard_map/while/body/eval_jaxpr/reduce_scatter | solution.py:64
  168.6 26.3 %reduce-scatter.2.cloned.1.call-start = ((), (), s32[]{:S(2)}) async-start(), calls=%async_computation.1 | async-start | bytes 368640 | tf_op jit(solution)/shard_map/while/body/eval_jaxpr/reduce_scatter | solution.py:64
  206.9 26.4 %reduce-scatter.2.cloned.1.call-start = ((), (), s32[]{:S(2)}) async-start(), calls=%async_computation.1 | async-start | bytes 368640 | tf_op jit(solution)/shard_map/while/body/eval_jaxpr/reduce_scatter | solution.py:64
  245.3 26.4 %reduce-scatter.2.cloned.1.call-start = ((), (), s32[]{:S(2)}) async-start(), calls=%async_computation.1 | async-start | bytes 368640 | tf_op jit(solution)/shard_map/while/body/eval_jaxpr/reduce_scatter | solution.py:64
  283.7 26.4 %reduce-scatter.2.cloned.1.call-start = ((), (), s32[]{:S(2)}) async-start(), calls=%async_computation.1 | async-start | bytes 368640 | tf_op jit(solution)/shard_map/while/body/eval_jaxpr/reduce_scatter | solution.py:64
  322.1 26.4 %reduce-scatter.2.cloned.1.call-start = ((), (), s32[]{:S(2)}) async-start(), calls=%async_computation.1 | async-start | bytes 368640 | tf_op jit(solution)/shard_map/while/body/eval_jaxpr/reduce_scatter | solution.py:64
  360.5 26.4 %reduce-scatter.2.cloned.1.call-start = ((), (), s32[]{:S(2)}) async-start(), calls=%async_computation.1 | async-start | bytes 368640 | tf_op jit(solution)/shard_map/while/body/eval_jaxpr/reduce_scatter | solution.py:64
  398.9 26.4 %reduce-scatter.2.cloned.1.call-start = ((), (), s32[]{:S(2)}) async-start(), calls=%async_computation.1 | async-start | bytes 368640 | tf_op jit(solution)/shard_map/while/body/eval_jaxpr/reduce_scatter | solution.py:64
  437.2 26.4 %reduce-scatter.2.cloned.1.call-start = ((), (), s32[]{:S(2)}) async-start(), calls=%async_computation.1 | async-start | bytes 368640 | tf_op jit(solution)/shard_map/while/body/eval_jaxpr/reduce_scatter | solution.py:64
  475.6 26.4 %reduce-scatter.2.cloned.1.call-start = ((), (), s32[]{:S(2)}) async-start(), calls=%async_computation.1 | async-start | bytes 368640 | tf_op jit(solution)/shard_map/while/body/eval_jaxpr/reduce_scatter | solution.py:64
  514.0 26.4 %reduce-scatter.2.cloned.1.call-start = ((), (), s32[]{:S(2)}) async-start(), calls=%async_computation.1 | async-start | bytes 368640 | tf_op jit(solution)/shard_map/while/body/eval_jaxpr/reduce_scatter | solution.py:64
  552.4 26.4 %reduce-scatter.2.cloned.1.call-start = ((), (), s32[]{:S(2)}) async-start(), calls=%async_computation.1 | async-start | bytes 368640 | tf_op jit(solution)/shard_map/while/body/eval_jaxpr/reduce_scatter | solution.py:64
  590.8 26.4 %reduce-scatter.2.cloned.1.call-start = ((), (), s32[]{:S(2)}) async-start(), calls=%async_computation.1 | async-start | bytes 368640 | tf_op jit(solution)/shard_map/while/body/eval_jaxpr/reduce_scatter | solution.py:64
  629.1 26.4 %reduce-scatter.2.cloned.1.call-start = ((), (), s32[]{:S(2)}) async-start(), calls=%async_computation.1 | async-start | bytes 368640 | tf_op jit(solution)/shard_map/while/body/eval_jaxpr/reduce_scatter | solution.py:64
  667.5 26.4 %reduce-scatter.2.cloned.1.call-start = ((), (), s32[]{:S(2)}) async-start(), calls=%async_computation.1 | async-start | bytes 368640 | tf_op jit(solution)/shard_map/while/body/eval_jaxpr/reduce_scatter | solution.py:64
  705.9 26.4 %reduce-scatter.2.cloned.1.call-start = ((), (), s32[]{:S(2)}) async-start(), calls=%async_computation.1 | async-start | bytes 368640 | tf_op jit(solution)/shard_map/while/body/eval_jaxpr/reduce_scatter | solution.py:64
  744.3 26.4 %reduce-scatter.2.cloned.1.call-start = ((), (), s32[]{:S(2)}) async-start(), calls=%async_computation.1 | async-start | bytes 368640 | tf_op jit(solution)/shard_map/while/body/eval_jaxpr/reduce_scatter | solution.py:64
  782.7 26.4 %reduce-scatter.2.cloned.1.call-start = ((), (), s32[]{:S(2)}) async-start(), calls=%async_computation.1 | async-start | bytes 368640 | tf_op jit(solution)/shard_map/while/body/eval_jaxpr/reduce_scatter | solution.py:64
  821.1 26.4 %reduce-scatter.2.cloned.1.call-start = ((), (), s32[]{:S(2)}) async-start(), calls=%async_computation.1 | async-start | bytes 368640 | tf_op jit(solution)/shard_map/while/body/eval_jaxpr/reduce_scatter | solution.py:64
  859.4 26.4 %reduce-scatter.2.cloned.1.call-start = ((), (), s32[]{:S(2)}) async-start(), calls=%async_computation.1 | async-start | bytes 368640 | tf_op jit(solution)/shard_map/while/body/eval_jaxpr/reduce_scatter | solution.py:64
  897.8 26.4 %reduce-scatter.2.cloned.1.call-start = ((), (), s32[]{:S(2)}) async-start(), calls=%async_computation.1 | async-start | bytes 368640 | tf_op jit(solution)/shard_map/while/body/eval_jaxpr/reduce_scatter | solution.py:64
  936.2 26.4 %reduce-scatter.2.cloned.1.call-start = ((), (), s32[]{:S(2)}) async-start(), calls=%async_computation.1 | async-start | bytes 368640 | tf_op jit(solution)/shard_map/while/body/eval_jaxpr/reduce_scatter | solution.py:64
  974.6 26.4 %reduce-scatter.2.cloned.1.call-start = ((), (), s32[]{:S(2)}) async-start(), calls=%async_computation.1 | async-start | bytes 368640 | tf_op jit(solution)/shard_map/while/body/eval_jaxpr/reduce_scatter | solution.py:64
  1013.0 26.4 %reduce-scatter.2.cloned.1.call-start = ((), (), s32[]{:S(2)}) async-start(), calls=%async_computation.1 | async-start | bytes 368640 | tf_op jit(solution)/shard_map/while/body/eval_jaxpr/reduce_scatter | solution.py:64
  1051.4 26.4 %reduce-scatter.2.cloned.1.call-start = ((), (), s32[]{:S(2)}) async-start(), calls=%async_computation.1 | async-start | bytes 368640 | tf_op jit(solution)/shard_map/while/body/eval_jaxpr/reduce_scatter | solution.py:64
  1089.7 26.4 %reduce-scatter.2.cloned.1.call-start = ((), (), s32[]{:S(2)}) async-start(), calls=%async_computation.1 | async-start | bytes 368640 | tf_op jit(solution)/shard_map/while/body/eval_jaxpr/reduce_scatter | solution.py:64
  1128.1 26.4 %reduce-scatter.2.cloned.1.call-start = ((), (), s32[]{:S(2)}) async-start(), calls=%async_computation.1 | async-start | bytes 368640 | tf_op jit(solution)/shard_map/while/body/eval_jaxpr/reduce_scatter | solution.py:64
  1166.5 26.4 %reduce-scatter.2.cloned.1.call-start = ((), (), s32[]{:S(2)}) async-start(), calls=%async_computation.1 | async-start | bytes 368640 | tf_op jit(solution)/shard_map/while/body/eval_jaxpr/reduce_scatter | solution.py:64
  1204.9 26.4 %reduce-scatter.2.cloned.1.call-start = ((), (), s32[]{:S(2)}) async-start(), calls=%async_computation.1 | async-start | bytes 368640 | tf_op jit(solution)/shard_map/while/body/eval_jaxpr/reduce_scatter | solution.py:64
  (96 other events, 1474.6 us)
Sparse Core Ops, SparseCore 0:
  21.9 19.4 reduce-scatter.1
  65.5 14.2 reduce-scatter.1
  103.9 14.2 reduce-scatter.1
  142.3 14.2 reduce-scatter.1
  180.6 14.2 reduce-scatter.1
  219.0 14.2 reduce-scatter.1
  257.4 14.2 reduce-scatter.1
  295.8 14.2 reduce-scatter.1
  334.2 14.2 reduce-scatter.1
  372.5 14.2 reduce-scatter.1
  410.9 14.2 reduce-scatter.1
  449.3 14.2 reduce-scatter.1
  487.7 14.2 reduce-scatter.1
  526.1 14.2 reduce-scatter.1
  564.5 14.2 reduce-scatter.1
  602.8 14.2 reduce-scatter.1
  641.2 14.2 reduce-scatter.1
  679.6 14.2 reduce-scatter.1
  718.0 14.2 reduce-scatter.1
  756.4 14.2 reduce-scatter.1
  794.8 14.2 reduce-scatter.1
  833.1 14.2 reduce-scatter.1
  871.5 14.2 reduce-scatter.1
  909.9 14.2 reduce-scatter.1
  948.3 14.2 reduce-scatter.1
  986.7 14.2 reduce-scatter.1
  1025.1 14.2 reduce-scatter.1
  1063.4 14.2 reduce-scatter.1
  1101.8 14.2 reduce-scatter.1
  1140.2 14.2 reduce-scatter.1
  1178.6 14.2 reduce-scatter.1
  1217.0 14.2 reduce-scatter.1
where the time goes:
time: 1260 us; the launch traced here: 1250 us
  waiting for transfers between devices  535 us (42%)
  matrix products  330 us (26%)
  blocking collectives  218 us (17%)
  starting transfers between devices  120 us (10%)
  other arithmetic  28.9 us (2%)
  between operations  14.4 us (1%)
    reduce_scatter x32, waiting for transfers between devices, step(): lax.psum_scatter(returned_grad_part.astype(jnp.bfloat16), 'blk', scatter_...  460 us
    all_gather x32, blocking collectives, step(): joined_tiles = lax.all_gather(tile_length, 'blk', axis=0, tiled=True)  218 us
    dot_general x32, matrix products, both_grads(): jnp.dot(loss_grid_scaled, tile_length, preferred_element_type=jnp.float32)  167 us
    dot_general x32, matrix products, remaining_factors(): lax.dot_general(visual_features, tile_length, (((1,), (1,)), ((), ())), p...  123 us
    ppermute x64, starting transfers between devices, passed_along(): lax.ppermute(array, axis, [(i, (i + by) % peers) for i in range(peers)])  120 us
    ppermute x64, waiting for transfers between devices, passed_along(): lax.ppermute(array, axis, [(i, (i + by) % peers) for i in range(peers)])  74.3 us
    dot_general x32, matrix products, both_grads(): lax.dot_general(loss_grid_scaled, visual_features, (((0,), (0,)), ((), ()...  40.1 us
    add x32, other arithmetic, step(): held + lax.psum_scatter(returned_grad_part.astype(jnp.bfloat16), 'blk', s...  28.8 us
  transfers between devices with their start and end apart: 96, of which 64 were waited for; matrix products, arithmetic and copies ran while one was open for 16% of the time, Pallas kernels for 0%

commit v1 on v0

--- a/solution.py
+++ b/solution.py
@@ -48,7 +48,8 @@
     def step(turn, carry):
         grad_img, tile_length, held = carry
         reference_offset = (wpos - turn) % n_wide
-        joined_tiles = lax.all_gather(tile_length, "blk", axis=0, tiled=True)
+        sent = jnp.stack([tile_length] * lax.axis_size("blk"))
+        joined_tiles = jnp.concatenate(lax.all_to_all(sent, "blk", 0, 0), axis=0)
         loss_grid_scaled = remaining_factors(
             visual_features,
             joined_tiles,

time: 1260 us -> 1400 us (1.11)
  blocking collectives: 218 us -> 0 us
  waiting for transfers between devices: 535 us -> 747 us
  starting transfers between devices: 120 us -> 252 us
  local copies, waits for them, and re-layouts: 1.91 us -> 25.1 us
    all_gather x32 -> x0, blocking collectives: 218 us -> none  [step(): joined_tiles = lax.all_gather(tile_length, 'blk', axis=0, tiled=True)]
    all_to_all x0 -> x32, waiting for transfers between devices: none -> 177 us  [step(): joined_tiles = jnp.concatenate(lax.all_to_all(sent, 'blk', 0, 0), axis=0)]
    all_to_all x0 -> x32, starting transfers between devices: none -> 144 us  [step(): joined_tiles = jnp.concatenate(lax.all_to_all(sent, 'blk', 0, 0), axis=0)]
    another operation x0 -> x32, local copies, waits for them, and re-layouts: none -> 23.2 us  [step(): sent = jnp.stack([tile_length] * lax.axis_size('blk'))]
    reduce_scatter x32, waiting for transfers between devices: 460 us -> 482 us  [step(): lax.psum_scatter(returned_grad_part.astype(jnp.bfloat16), 'blk', scatter_...]
  transfers between devices with their start and end apart: 96 -> 128, of which waited for: 64 -> 96; matrix products, arithmetic and copies ran while one was open for 16% -> 14% of each run, Pallas kernels for 0% -> 0%
where the time goes in v1:
time: 1400 us
  waiting for transfers between devices  747 us (53%)
  matrix products  329 us (24%)
  starting transfers between devices  252 us (18%)
  other arithmetic  28.9 us (2%)
  local copies, waits for them, and re-layouts  25.1 us (2%)
  between operations  14.4 us (1%)
    reduce_scatter x32, waiting for transfers between devices, step(): lax.psum_scatter(returned_grad_part.astype(jnp.bfloat16), 'blk', scatter_...  482 us
    all_to_all x32, waiting for transfers between devices, step(): joined_tiles = jnp.concatenate(lax.all_to_all(sent, 'blk', 0, 0), axis=0)  177 us
    dot_general x32, matrix products, both_grads(): jnp.dot(loss_grid_scaled, tile_length, preferred_element_type=jnp.float32)  167 us
    all_to_all x32, starting transfers between devices, step(): joined_tiles = jnp.concatenate(lax.all_to_all(sent, 'blk', 0, 0), axis=0)  144 us
    dot_general x32, matrix products, remaining_factors(): lax.dot_general(visual_features, tile_length, (((1,), (1,)), ((), ())), p...  123 us
    ppermute x64, starting transfers between devices, passed_along(): lax.ppermute(array, axis, [(i, (i + by) % peers) for i in range(peers)])  108 us
    ppermute x64, waiting for transfers between devices, passed_along(): lax.ppermute(array, axis, [(i, (i + by) % peers) for i in range(peers)])  88 us
    dot_general x32, matrix products, both_grads(): lax.dot_general(loss_grid_scaled, visual_features, (((0,), (0,)), ((), ()...  39.9 us
  transfers between devices with their start and end apart: 128, of which 96 were waited for; matrix products, arithmetic and copies ran while one was open for 14% of the time, Pallas kernels for 0%

profile of v1, /device:TPU:1, one launch (start us, length us, event | category | flops | bytes accessed | tf_op | source)
XLA Modules:
  0.0 1397.9 jit_solution(13251434701911759520)
XLA Ops:
  8.7 1382.0 %while.20 = (s32[]{:T(128)}, f32[1024,1152]{1,0:T(8,128)}, bf16[32,1152]{1,0:T(8,128)(2,1)S(1)}, f32[32,1152]{1,0:T(8,128)S(1)}, f32[]{:T(128)}, /*index=5*/s32[...) while((s32[]{:T(128)}, f32[1024,1152]{1,0:T(8,128)}, ...), condition=%wide.region_2.3_spmd.clone, body=%wide.region_0.2_spmd.clone.sunk | while | flops 910123136 | bytes 29029856 | solution.py:73
  28.9 16.9 %reduce-scatter.2.cloned.1.call-done = bf16[32,1152]{1,0:T(8,128)(2,1)} async-done(((bf16[128,1152]{1,0:T(8,128)(2,1)}), bf16[32,1152]{1,0:T(8,128)(2,1)}) %reduce-scatter.2.cloned.1.call-update) | async-done | bytes 73744 | tf_op jit(solution)/shard_map/while/body/eval_jaxpr/reduce_scatter | solution.py:65
  73.8 15.0 %reduce-scatter.2.cloned.1.call-done = bf16[32,1152]{1,0:T(8,128)(2,1)} async-done(((bf16[128,1152]{1,0:T(8,128)(2,1)}), bf16[32,1152]{1,0:T(8,128)(2,1)}) %reduce-scatter.2.cloned.1.call-update) | async-done | bytes 73744 | tf_op jit(solution)/shard_map/while/body/eval_jaxpr/reduce_scatter | solution.py:65
  116.8 15.0 %reduce-scatter.2.cloned.1.call-done = bf16[32,1152]{1,0:T(8,128)(2,1)} async-done(((bf16[128,1152]{1,0:T(8,128)(2,1)}), bf16[32,1152]{1,0:T(8,128)(2,1)}) %reduce-scatter.2.cloned.1.call-update) | async-done | bytes 73744 | tf_op jit(solution)/shard_map/while/body/eval_jaxpr/reduce_scatter | solution.py:65
  159.7 15.0 %reduce-scatter.2.cloned.1.call-done = bf16[32,1152]{1,0:T(8,128)(2,1)} async-done(((bf16[128,1152]{1,0:T(8,128)(2,1)}), bf16[32,1152]{1,0:T(8,128)(2,1)}) %reduce-scatter.2.cloned.1.call-update) | async-done | bytes 73744 | tf_op jit(solution)/shard_map/while/body/eval_jaxpr/reduce_scatter | solution.py:65
  202.8 15.0 %reduce-scatter.2.cloned.1.call-done = bf16[32,1152]{1,0:T(8,128)(2,1)} async-done(((bf16[128,1152]{1,0:T(8,128)(2,1)}), bf16[32,1152]{1,0:T(8,128)(2,1)}) %reduce-scatter.2.cloned.1.call-update) | async-done | bytes 73744 | tf_op jit(solution)/shard_map/while/body/eval_jaxpr/reduce_scatter | solution.py:65
  245.7 15.0 %reduce-scatter.2.cloned.1.call-done = bf16[32,1152]{1,0:T(8,128)(2,1)} async-done(((bf16[128,1152]{1,0:T(8,128)(2,1)}), bf16[32,1152]{1,0:T(8,128)(2,1)}) %reduce-scatter.2.cloned.1.call-update) | async-done | bytes 73744 | tf_op jit(solution)/shard_map/while/body/eval_jaxpr/reduce_scatter | solution.py:65
  288.7 15.0 %reduce-scatter.2.cloned.1.call-done = bf16[32,1152]{1,0:T(8,128)(2,1)} async-done(((bf16[128,1152]{1,0:T(8,128)(2,1)}), bf16[32,1152]{1,0:T(8,128)(2,1)}) %reduce-scatter.2.cloned.1.call-update) | async-done | bytes 73744 | tf_op jit(solution)/shard_map/while/body/eval_jaxpr/reduce_scatter | solution.py:65
  331.8 14.9 %reduce-scatter.2.cloned.1.call-done = bf16[32,1152]{1,0:T(8,128)(2,1)} async-done(((bf16[128,1152]{1,0:T(8,128)(2,1)}), bf16[32,1152]{1,0:T(8,128)(2,1)}) %reduce-scatter.2.cloned.1.call-update) | async-done | bytes 73744 | tf_op jit(solution)/shard_map/while/body/eval_jaxpr/reduce_scatter | solution.py:65
  374.7 15.0 %reduce-scatter.2.cloned.1.call-done = bf16[32,1152]{1,0:T(8,128)(2,1)} async-done(((bf16[128,1152]{1,0:T(8,128)(2,1)}), bf16[32,1152]{1,0:T(8,128)(2,1)}) %reduce-scatter.2.cloned.1.call-update) | async-done | bytes 73744 | tf_op jit(solution)/shard_map/while/body/eval_jaxpr/reduce_scatter | solution.py:65
  417.7 15.0 %reduce-scatter.2.cloned.1.call-done = bf16[32,1152]{1,0:T(8,128)(2,1)} async-done(((bf16[128,1152]{1,0:T(8,128)(2,1)}), bf16[32,1152]{1,0:T(8,128)(2,1)}) %reduce-scatter.2.cloned.1.call-update) | async-done | bytes 73744 | tf_op jit(solution)/shard_map/while/body/eval_jaxpr/reduce_scatter | solution.py:65
  460.7 15.0 %reduce-scatter.2.cloned.1.call-done = bf16[32,1152]{1,0:T(8,128)(2,1)} async-done(((bf16[128,1152]{1,0:T(8,128)(2,1)}), bf16[32,1152]{1,0:T(8,128)(2,1)}) %reduce-scatter.2.cloned.1.call-update) | async-done | bytes 73744 | tf_op jit(solution)/shard_map/while/body/eval_jaxpr/reduce_scatter | solution.py:65
  503.8 15.0 %reduce-scatter.2.cloned.1.call-done = bf16[32,1152]{1,0:T(8,128)(2,1)} async-done(((bf16[128,1152]{1,0:T(8,128)(2,1)}), bf16[32,1152]{1,0:T(8,128)(2,1)}) %reduce-scatter.2.cloned.1.call-update) | async-done | bytes 73744 | tf_op jit(solution)/shard_map/while/body/eval_jaxpr/reduce_scatter | solution.py:65
  546.7 15.0 %reduce-scatter.2.cloned.1.call-done = bf16[32,1152]{1,0:T(8,128)(2,1)} async-done(((bf16[128,1152]{1,0:T(8,128)(2,1)}), bf16[32,1152]{1,0:T(8,128)(2,1)}) %reduce-scatter.2.cloned.1.call-update) | async-done | bytes 73744 | tf_op jit(solution)/shard_map/while/body/eval_jaxpr/reduce_scatter | solution.py:65
  589.8 14.9 %reduce-scatter.2.cloned.1.call-done = bf16[32,1152]{1,0:T(8,128)(2,1)} async-done(((bf16[128,1152]{1,0:T(8,128)(2,1)}), bf16[32,1152]{1,0:T(8,128)(2,1)}) %reduce-scatter.2.cloned.1.call-update) | async-done | bytes 73744 | tf_op jit(solution)/shard_map/while/body/eval_jaxpr/reduce_scatter | solution.py:65
  632.7 15.0 %reduce-scatter.2.cloned.1.call-done = bf16[32,1152]{1,0:T(8,128)(2,1)} async-done(((bf16[128,1152]{1,0:T(8,128)(2,1)}), bf16[32,1152]{1,0:T(8,128)(2,1)}) %reduce-scatter.2.cloned.1.call-update) | async-done | bytes 73744 | tf_op jit(solution)/shard_map/while/body/eval_jaxpr/reduce_scatter | solution.py:65
  675.7 15.0 %reduce-scatter.2.cloned.1.call-done = bf16[32,1152]{1,0:T(8,128)(2,1)} async-done(((bf16[128,1152]{1,0:T(8,128)(2,1)}), bf16[32,1152]{1,0:T(8,128)(2,1)}) %reduce-scatter.2.cloned.1.call-update) | async-done | bytes 73744 | tf_op jit(solution)/shard_map/while/body/eval_jaxpr/reduce_scatter | solution.py:65
  718.8 14.9 %reduce-scatter.2.cloned.1.call-done = bf16[32,1152]{1,0:T(8,128)(2,1)} async-done(((bf16[128,1152]{1,0:T(8,128)(2,1)}), bf16[32,1152]{1,0:T(8,128)(2,1)}) %reduce-scatter.2.cloned.1.call-update) | async-done | bytes 73744 | tf_op jit(solution)/shard_map/while/body/eval_jaxpr/reduce_scatter | solution.py:65
  761.7 15.0 %reduce-scatter.2.cloned.1.call-done = bf16[32,1152]{1,0:T(8,128)(2,1)} async-done(((bf16[128,1152]{1,0:T(8,128)(2,1)}), bf16[32,1152]{1,0:T(8,128)(2,1)}) %reduce-scatter.2.cloned.1.call-update) | async-done | bytes 73744 | tf_op jit(solution)/shard_map/while/body/eval_jaxpr/reduce_scatter | solution.py:65
  804.7 15.0 %reduce-scatter.2.cloned.1.call-done = bf16[32,1152]{1,0:T(8,128)(2,1)} async-done(((bf16[128,1152]{1,0:T(8,128)(2,1)}), bf16[32,1152]{1,0:T(8,128)(2,1)}) %reduce-scatter.2.cloned.1.call-update) | async-done | bytes 73744 | tf_op jit(solution)/shard_map/while/body/eval_jaxpr/reduce_scatter | solution.py:65
  847.8 14.9 %reduce-scatter.2.cloned.1.call-done = bf16[32,1152]{1,0:T(8,128)(2,1)} async-done(((bf16[128,1152]{1,0:T(8,128)(2,1)}), bf16[32,1152]{1,0:T(8,128)(2,1)}) %reduce-scatter.2.cloned.1.call-update) | async-done | bytes 73744 | tf_op jit(solution)/shard_map/while/body/eval_jaxpr/reduce_scatter | solution.py:65
  890.7 15.0 %reduce-scatter.2.cloned.1.call-done = bf16[32,1152]{1,0:T(8,128)(2,1)} async-done(((bf16[128,1152]{1,0:T(8,128)(2,1)}), bf16[32,1152]{1,0:T(8,128)(2,1)}) %reduce-scatter.2.cloned.1.call-update) | async-done | bytes 73744 | tf_op jit(solution)/shard_map/while/body/eval_jaxpr/reduce_scatter | solution.py:65
  933.7 15.0 %reduce-scatter.2.cloned.1.call-done = bf16[32,1152]{1,0:T(8,128)(2,1)} async-done(((bf16[128,1152]{1,0:T(8,128)(2,1)}), bf16[32,1152]{1,0:T(8,128)(2,1)}) %reduce-scatter.2.cloned.1.call-update) | async-done | bytes 73744 | tf_op jit(solution)/shard_map/while/body/eval_jaxpr/reduce_scatter | solution.py:65
  976.7 14.9 %reduce-scatter.2.cloned.1.call-done = bf16[32,1152]{1,0:T(8,128)(2,1)} async-done(((bf16[128,1152]{1,0:T(8,128)(2,1)}), bf16[32,1152]{1,0:T(8,128)(2,1)}) %reduce-scatter.2.cloned.1.call-update) | async-done | bytes 73744 | tf_op jit(solution)/shard_map/while/body/eval_jaxpr/reduce_scatter | solution.py:65
  1019.7 15.0 %reduce-scatter.2.cloned.1.call-done = bf16[32,1152]{1,0:T(8,128)(2,1)} async-done(((bf16[128,1152]{1,0:T(8,128)(2,1)}), bf16[32,1152]{1,0:T(8,128)(2,1)}) %reduce-scatter.2.cloned.1.call-update) | async-done | bytes 73744 | tf_op jit(solution)/shard_map/while/body/eval_jaxpr/reduce_scatter | solution.py:65
  1062.7 15.0 %reduce-scatter.2.cloned.1.call-done = bf16[32,1152]{1,0:T(8,128)(2,1)} async-done(((bf16[128,1152]{1,0:T(8,128)(2,1)}), bf16[32,1152]{1,0:T(8,128)(2,1)}) %reduce-scatter.2.cloned.1.call-update) | async-done | bytes 73744 | tf_op jit(solution)/shard_map/while/body/eval_jaxpr/reduce_scatter | solution.py:65
  1148.7 15.0 %reduce-scatter.2.cloned.1.call-done = bf16[32,1152]{1,0:T(8,128)(2,1)} async-done(((bf16[128,1152]{1,0:T(8,128)(2,1)}), bf16[32,1152]{1,0:T(8,128)(2,1)}) %reduce-scatter.2.cloned.1.call-update) | async-done | bytes 73744 | tf_op jit(solution)/shard_map/while/body/eval_jaxpr/reduce_scatter | solution.py:65
  1191.7 15.0 %reduce-scatter.2.cloned.1.call-done = bf16[32,1152]{1,0:T(8,128)(2,1)} async-done(((bf16[128,1152]{1,0:T(8,128)(2,1)}), bf16[32,1152]{1,0:T(8,128)(2,1)}) %reduce-scatter.2.cloned.1.call-update) | async-done | bytes 73744 | tf_op jit(solution)/shard_map/while/body/eval_jaxpr/reduce_scatter | solution.py:65
  1234.7 14.9 %reduce-scatter.2.cloned.1.call-done = bf16[32,1152]{1,0:T(8,128)(2,1)} async-done(((bf16[128,1152]{1,0:T(8,128)(2,1)}), bf16[32,1152]{1,0:T(8,128)(2,1)}) %reduce-scatter.2.cloned.1.call-update) | async-done | bytes 73744 | tf_op jit(solution)/shard_map/while/body/eval_jaxpr/reduce_scatter | solution.py:65
  1277.7 15.0 %reduce-scatter.2.cloned.1.call-done = bf16[32,1152]{1,0:T(8,128)(2,1)} async-done(((bf16[128,1152]{1,0:T(8,128)(2,1)}), bf16[32,1152]{1,0:T(8,128)(2,1)}) %reduce-scatter.2.cloned.1.call-update) | async-done | bytes 73744 | tf_op jit(solution)/shard_map/while/body/eval_jaxpr/reduce_scatter | solution.py:65
  1320.7 15.0 %reduce-scatter.2.cloned.1.call-done = bf16[32,1152]{1,0:T(8,128)(2,1)} async-done(((bf16[128,1152]{1,0:T(8,128)(2,1)}), bf16[32,1152]{1,0:T(8,128)(2,1)}) %reduce-scatter.2.cloned.1.call-update) | async-done | bytes 73744 | tf_op jit(solution)/shard_map/while/body/eval_jaxpr/reduce_scatter | solution.py:65
  1363.7 14.9 %reduce-scatter.2.cloned.1.call-done = bf16[32,1152]{1,0:T(8,128)(2,1)} async-done(((bf16[128,1152]{1,0:T(8,128)(2,1)}), bf16[32,1152]{1,0:T(8,128)(2,1)}) %reduce-scatter.2.cloned.1.call-update) | async-done | bytes 73744 | tf_op jit(solution)/shard_map/while/body/eval_jaxpr/reduce_scatter | solution.py:65
  (549 shorter events, 914.9 us)
Async XLA Ops:
  14.5 31.3 %reduce-scatter.2.cloned.1.call-start = ((), (), s32[]{:S(2)}) async-start(), calls=%async_computation.2 | async-start | bytes 368640 | tf_op jit(solution)/shard_map/while/body/eval_jaxpr/reduce_scatter | solution.py:65
  25.1 27.2 %collective-permute-start = (bf16[32,1152]{1,0:T(8,128)(2,1)S(1)}, bf16[32,1152]{1,0:T(8,128)(2,1)S(1)}, u32[]{:S(2)}, u32[]{:S(2)}) collective-permute-start(bf16[32,1152]{1,0:T(8,128)(2,1)S(1)} %copy.13), channel_id=1, source_target_pairs={{0,4},{4,8},{8,12},{12,16},{16,20},{20,24},{24,28},{28,32},{32,36}... | collective-permute-start | bytes 221192 | tf_op jit(solution)/shard_map/while/body/eval_jaxpr/ppermute | solution.py:9
  63.0 25.7 %reduce-scatter.2.cloned.1.call-start = ((), (), s32[]{:S(2)}) async-start(), calls=%async_computation.2 | async-start | bytes 368640 | tf_op jit(solution)/shard_map/while/body/eval_jaxpr/reduce_scatter | solution.py:65
  106.0 25.7 %reduce-scatter.2.cloned.1.call-start = ((), (), s32[]{:S(2)}) async-start(), calls=%async_computation.2 | async-start | bytes 368640 | tf_op jit(solution)/shard_map/while/body/eval_jaxpr/reduce_scatter | solution.py:65
  149.0 25.8 %reduce-scatter.2.cloned.1.call-start = ((), (), s32[]{:S(2)}) async-start(), calls=%async_computation.2 | async-start | bytes 368640 | tf_op jit(solution)/shard_map/while/body/eval_jaxpr/reduce_scatter | solution.py:65
  192.0 25.7 %reduce-scatter.2.cloned.1.call-start = ((), (), s32[]{:S(2)}) async-start(), calls=%async_computation.2 | async-start | bytes 368640 | tf_op jit(solution)/shard_map/while/body/eval_jaxpr/reduce_scatter | solution.py:65
  235.0 25.7 %reduce-scatter.2.cloned.1.call-start = ((), (), s32[]{:S(2)}) async-start(), calls=%async_computation.2 | async-start | bytes 368640 | tf_op jit(solution)/shard_map/while/body/eval_jaxpr/reduce_scatter | solution.py:65
  278.0 25.8 %reduce-scatter.2.cloned.1.call-start = ((), (), s32[]{:S(2)}) async-start(), calls=%async_computation.2 | async-start | bytes 368640 | tf_op jit(solution)/shard_map/while/body/eval_jaxpr/reduce_scatter | solution.py:65
  321.0 25.7 %reduce-scatter.2.cloned.1.call-start = ((), (), s32[]{:S(2)}) async-start(), calls=%async_computation.2 | async-start | bytes 368640 | tf_op jit(solution)/shard_map/while/body/eval_jaxpr/reduce_scatter | solution.py:65
  364.0 25.8 %reduce-scatter.2.cloned.1.call-start = ((), (), s32[]{:S(2)}) async-start(), calls=%async_computation.2 | async-start | bytes 368640 | tf_op jit(solution)/shard_map/while/body/eval_jaxpr/reduce_scatter | solution.py:65
  407.0 25.8 %reduce-scatter.2.cloned.1.call-start = ((), (), s32[]{:S(2)}) async-start(), calls=%async_computation.2 | async-start | bytes 368640 | tf_op jit(solution)/shard_map/while/body/eval_jaxpr/reduce_scatter | solution.py:65
  450.0 25.7 %reduce-scatter.2.cloned.1.call-start = ((), (), s32[]{:S(2)}) async-start(), calls=%async_computation.2 | async-start | bytes 368640 | tf_op jit(solution)/shard_map/while/body/eval_jaxpr/reduce_scatter | solution.py:65
  493.0 25.7 %reduce-scatter.2.cloned.1.call-start = ((), (), s32[]{:S(2)}) async-start(), calls=%async_computation.2 | async-start | bytes 368640 | tf_op jit(solution)/shard_map/while/body/eval_jaxpr/reduce_scatter | solution.py:65
  536.0 25.8 %reduce-scatter.2.cloned.1.call-start = ((), (), s32[]{:S(2)}) async-start(), calls=%async_computation.2 | async-start | bytes 368640 | tf_op jit(solution)/shard_map/while/body/eval_jaxpr/reduce_scatter | solution.py:65
  579.0 25.7 %reduce-scatter.2.cloned.1.call-start = ((), (), s32[]{:S(2)}) async-start(), calls=%async_computation.2 | async-start | bytes 368640 | tf_op jit(solution)/shard_map/while/body/eval_jaxpr/reduce_scatter | solution.py:65
  622.0 25.8 %reduce-scatter.2.cloned.1.call-start = ((), (), s32[]{:S(2)}) async-start(), calls=%async_computation.2 | async-start | bytes 368640 | tf_op jit(solution)/shard_map/while/body/eval_jaxpr/reduce_scatter | solution.py:65
  665.0 25.8 %reduce-scatter.2.cloned.1.call-start = ((), (), s32[]{:S(2)}) async-start(), calls=%async_computation.2 | async-start | bytes 368640 | tf_op jit(solution)/shard_map/while/body/eval_jaxpr/reduce_scatter | solution.py:65
  708.0 25.7 %reduce-scatter.2.cloned.1.call-start = ((), (), s32[]{:S(2)}) async-start(), calls=%async_computation.2 | async-start | bytes 368640 | tf_op jit(solution)/shard_map/while/body/eval_jaxpr/reduce_scatter | solution.py:65
  751.0 25.8 %reduce-scatter.2.cloned.1.call-start = ((), (), s32[]{:S(2)}) async-start(), calls=%async_computation.2 | async-start | bytes 368640 | tf_op jit(solution)/shard_map/while/body/eval_jaxpr/reduce_scatter | solution.py:65
  794.0 25.8 %reduce-scatter.2.cloned.1.call-start = ((), (), s32[]{:S(2)}) async-start(), calls=%async_computation.2 | async-start | bytes 368640 | tf_op jit(solution)/shard_map/while/body/eval_jaxpr/reduce_scatter | solution.py:65
  837.0 25.7 %reduce-scatter.2.cloned.1.call-start = ((), (), s32[]{:S(2)}) async-start(), calls=%async_computation.2 | async-start | bytes 368640 | tf_op jit(solution)/shard_map/while/body/eval_jaxpr/reduce_scatter | solution.py:65
  879.9 25.8 %reduce-scatter.2.cloned.1.call-start = ((), (), s32[]{:S(2)}) async-start(), calls=%async_computation.2 | async-start | bytes 368640 | tf_op jit(solution)/shard_map/while/body/eval_jaxpr/reduce_scatter | solution.py:65
  923.0 25.8 %reduce-scatter.2.cloned.1.call-start = ((), (), s32[]{:S(2)}) async-start(), calls=%async_computation.2 | async-start | bytes 368640 | tf_op jit(solution)/shard_map/while/body/eval_jaxpr/reduce_scatter | solution.py:65
  966.0 25.7 %reduce-scatter.2.cloned.1.call-start = ((), (), s32[]{:S(2)}) async-start(), calls=%async_computation.2 | async-start | bytes 368640 | tf_op jit(solution)/shard_map/while/body/eval_jaxpr/reduce_scatter | solution.py:65
  1008.9 25.8 %reduce-scatter.2.cloned.1.call-start = ((), (), s32[]{:S(2)}) async-start(), calls=%async_computation.2 | async-start | bytes 368640 | tf_op jit(solution)/shard_map/while/body/eval_jaxpr/reduce_scatter | solution.py:65
  1052.0 25.8 %reduce-scatter.2.cloned.1.call-start = ((), (), s32[]{:S(2)}) async-start(), calls=%async_computation.2 | async-start | bytes 368640 | tf_op jit(solution)/shard_map/while/body/eval_jaxpr/reduce_scatter | solution.py:65
  1137.9 25.8 %reduce-scatter.2.cloned.1.call-start = ((), (), s32[]{:S(2)}) async-start(), calls=%async_computation.2 | async-start | bytes 368640 | tf_op jit(solution)/shard_map/while/body/eval_jaxpr/reduce_scatter | solution.py:65
  1180.9 25.8 %reduce-scatter.2.cloned.1.call-start = ((), (), s32[]{:S(2)}) async-start(), calls=%async_computation.2 | async-start | bytes 368640 | tf_op jit(solution)/shard_map/while/body/eval_jaxpr/reduce_scatter | solution.py:65
  1224.0 25.7 %reduce-scatter.2.cloned.1.call-start = ((), (), s32[]{:S(2)}) async-start(), calls=%async_computation.2 | async-start | bytes 368640 | tf_op jit(solution)/shard_map/while/body/eval_jaxpr/reduce_scatter | solution.py:65
  1266.9 25.8 %reduce-scatter.2.cloned.1.call-start = ((), (), s32[]{:S(2)}) async-start(), calls=%async_computation.2 | async-start | bytes 368640 | tf_op jit(solution)/shard_map/while/body/eval_jaxpr/reduce_scatter | solution.py:65
  1309.9 25.8 %reduce-scatter.2.cloned.1.call-start = ((), (), s32[]{:S(2)}) async-start(), calls=%async_computation.2 | async-start | bytes 368640 | tf_op jit(solution)/shard_map/while/body/eval_jaxpr/reduce_scatter | solution.py:65
  1353.0 25.7 %reduce-scatter.2.cloned.1.call-start = ((), (), s32[]{:S(2)}) async-start(), calls=%async_computation.2 | async-start | bytes 368640 | tf_op jit(solution)/shard_map/while/body/eval_jaxpr/reduce_scatter | solution.py:65
  (128 other events, 1928.4 us)
Sparse Core Ops, SparseCore 0:
  25.2 20.4 reduce-scatter.1
  73.8 14.9 reduce-scatter.1
  116.8 14.9 reduce-scatter.1
  159.8 14.9 reduce-scatter.1
  202.8 14.8 reduce-scatter.1
  245.8 14.9 reduce-scatter.1
  288.8 14.9 reduce-scatter.1
  331.8 14.8 reduce-scatter.1
  374.7 14.9 reduce-scatter.1
  417.8 14.9 reduce-scatter.1
  460.8 14.9 reduce-scatter.1
  503.8 14.8 reduce-scatter.1
  546.8 14.9 reduce-scatter.1
  589.8 14.8 reduce-scatter.1
  632.7 14.9 reduce-scatter.1
  675.7 14.9 reduce-scatter.1
  718.8 14.8 reduce-scatter.1
  761.7 14.9 reduce-scatter.1
  804.7 14.9 reduce-scatter.1
  847.8 14.8 reduce-scatter.1
  890.7 14.9 reduce-scatter.1
  933.7 14.9 reduce-scatter.1
  976.8 14.8 reduce-scatter.1
  1019.7 14.9 reduce-scatter.1
  1062.7 14.9 reduce-scatter.1
  1105.8 14.8 reduce-scatter.1
  1148.7 14.9 reduce-scatter.1
  1191.7 14.9 reduce-scatter.1
  1234.8 14.8 reduce-scatter.1
  1277.7 14.9 reduce-scatter.1
  1320.7 14.9 reduce-scatter.1
  1363.8 14.8 reduce-scatter.1
